TPU v7x, 1024 devices: a whole 8x8x8 slice. The times are simulated.
1024 devices in a mesh: dp: 64 (over z_lo, x, core), mp: 16 (over y, z_hi).
Axes of the slice: x: 8, y: 8, z: 8 (z_hi: 2, z_lo: 4; z = z_hi * 4 + z_lo), core: 2. Of those that a mesh axis runs over, the one named last changes fastest.
Arguments:
- patches: bfloat16 [8192, 3072], P('dp', 'mp'), may hold values from -16 to 16
- pre_act: bfloat16 [8192, 12288], P('dp', 'mp'), may hold values from -6 to 6
- cotangent: bfloat16 [8192, 3072], P('dp', 'mp'), may hold values from -16 to 16
- w_up: bfloat16 [3072, 12288], P(None, 'mp'), may hold values from -0.109375 to 0.109375
- w_down: bfloat16 [12288, 3072], P('mp'), may hold values from -0.0546875 to 0.0546875
Outputs:
- grad_patches: bfloat16 [8192, 3072], P('dp', 'mp')
- grad_up: float32 [3072, 12288], P('dp', 'mp')
All inputs are finite; a program needn't handle non-finite values.
Results may differ from a plain program's by a relative error of at most 0.013.
Values may be sent and summed in bfloat16 or wider, within the bound.
A program may use at most 64 MiB of HBM per device.

v0:
```python
import math

import jax
import jax.numpy as jnp
from jax import lax
from jax.sharding import PartitionSpec as P


def gelu_slope(value):
    cdf_part = 0.5 * (1.0 + lax.erf(value * (1.0 / math.sqrt(2.0))))
    density = jnp.exp(-0.5 * value * value) * (1.0 / math.sqrt(2.0 * math.pi))
    return cdf_part + value * density


def per_device(patches, pre_act, cotangent, w_up, w_down):
    whole = lax.all_gather(patches, "mp", axis=1, tiled=True)
    width = whole.shape[1]
    values = whole.astype(jnp.float32)
    centre = jnp.mean(values, axis=1, keepdims=True)
    spread = values - centre
    inv_std = lax.rsqrt(jnp.mean(spread * spread, axis=1, keepdims=True) + 1e-06)
    unit = spread * inv_std
    normed = unit.astype(jnp.bfloat16)
    tokens_here = cotangent.shape[0]
    factor = 1.0 / math.sqrt(tokens_here * lax.axis_size("dp"))
    grad_act = lax.dot_general(
        lax.all_gather(cotangent, "mp", axis=1, tiled=True),
        w_down,
        (((1,), (1,)), ((), ())),
        preferred_element_type=jnp.float32,
    )
    grad_pre = (grad_act * gelu_slope(pre_act.astype(jnp.float32))).astype(jnp.bfloat16)
    local_width = width // lax.axis_size("mp")
    partial_sum = lax.dot_general(
        w_up, grad_pre, (((1,), (1,)), ((), ())), preferred_element_type=jnp.float32
    )
    rounded = lax.optimization_barrier(partial_sum.astype(jnp.bfloat16))
    grad_share = lax.psum_scatter(
        rounded.astype(jnp.float32).astype(jnp.bfloat16), "mp", scatter_dimension=0, tiled=True
    ).astype(jnp.float32)
    grad_norm = grad_share.T
    unit_local = lax.dynamic_slice_in_dim(unit, lax.axis_index("mp") * local_width, local_width, 1)
    first, second = lax.psum(
        (jnp.sum(grad_norm, axis=1), jnp.sum(grad_norm * unit_local, axis=1)), "mp"
    )
    result = cotangent.astype(jnp.float32) + inv_std * (
        grad_norm - first[:, None] / width - unit_local * second[:, None] / width
    )
    up_share = lax.psum_scatter(
        lax.dot_general(
            normed, grad_pre, (((0,), (0,)), ((), ())), preferred_element_type=jnp.float32
        )
        * factor,
        "dp",
        scatter_dimension=0,
        tiled=True,
    )
    return (result.astype(jnp.bfloat16), up_share)


def solution(mesh):
    return jax.shard_map(
        per_device,
        mesh=mesh,
        in_specs=(P("dp", "mp"), P("dp", "mp"), P("dp", "mp"), P(None, "mp"), P("mp", None)),
        out_specs=(P("dp", "mp"), P("dp", "mp")),
        check_vma=False,
    )
```

profile of v0, /device:TPU:32, one launch (start us, length us, event | category | flops | bytes accessed | tf_op | source)
XLA Modules:
  0.0 638.6 jit_solution(13713599487251559736)
XLA Ops:
  7.2 0.0 reduce-scatter.7.cloned.1.call-start
  7.2 79.4 %all_gather.7 = bf16[128,3072]{0,1:T(8,128)(2,1)S(1)} all-gather(bf16[128,192]{0,1:T(8,128)(2,1)} %param.7), channel_id=1, replica_groups=mesh['dp'=64,'mp'=16] {'mp'}, dimensions={1}, use_global_device_ids=true | all-gather | bytes 835584 | tf_op jit(solution)/shard_map/all_gather | solution.py:27
  86.6 0.0 copy-start
  86.6 4.2 fusion.4
  90.8 0.0 copy-done
  90.8 1.6 fusion
  92.5 0.0 copy-start.2
  92.5 1.2 copy.11
  93.7 0.0 reduce-scatter.7.cloned.1.call-update
  93.7 0.0 reduce-scatter.5.cloned.1.call-start
  93.7 0.0 copy-done.2
  93.7 67.0 %all_gather.6 = bf16[128,3072]{0,1:T(8,128)(2,1)S(1)} all-gather(bf16[128,192]{0,1:T(8,128)(2,1)S(1)} %copy-done.2), channel_id=1, replica_groups=mesh['dp'=64,'mp'=16] {'mp'}, dimensions={1}, use_global_device_ids=true | all-gather | bytes 835584 | tf_op jit(solution)/shard_map/all_gather | solution.py:16
  160.7 0.4 convert_reduce_fusion
  161.1 0.4 fusion.3
  161.6 5.0 convolution_multiply_fusion
  166.6 0.0 reduce-scatter.5.cloned.1.call-update
  166.6 0.0 copy-start.1
  166.6 0.2 fusion.1
  166.8 166.0 %reduce-scatter.7.cloned.1.call-done = bf16[192,128]{1,0:T(8,128)(2,1)} async-done(((bf16[3072,128]{1,0:T(8,128)(2,1)}), bf16[192,128]{1,0:T(8,128)(2,1)}) %reduce-scatter.7.cloned.1.call-update) | async-done | bytes 49168 | tf_op jit(solution)/shard_map/reduce_scatter | solution.py:38
  332.8 0.8 convert_reduce_fusion.1
  333.6 0.8 fusion.19
  334.5 45.8 %all-reduce = (f32[128]{0:T(128)S(1)}, f32[128]{0:T(128)S(1)}) all-reduce(f32[128]{0:T(128)S(1)} %fusion.19, f32[128]{0:T(128)S(1)} %convert_reduce_fusion.1), channel_id=1, replica_groups=mesh['dp'=64,'mp'=16] {'mp'}, use_global_device_ids=true, to_apply=%region_6.0 | all-reduce | flops 256 | bytes 2048 | tf_op jit(solution)/shard_map/psum | solution.py:43
  380.3 0.0 copy-done.1
  380.3 1.5 fusion.18
  381.8 250.0 %reduce-scatter.5.cloned.1.call-done = f32[48,768]{1,0:T(8,128)} async-done(((f32[3072,768]{1,0:T(8,128)}), f32[48,768]{1,0:T(8,128)}) %reduce-scatter.5.cloned.1.call-update) | async-done | bytes 147472 | tf_op jit(solution)/shard_map/reduce_scatter | solution.py:49
  (3 shorter events, 0.0 us)
Async XLA Ops:
  7.2 325.6 %reduce-scatter.7.cloned.1.call-start = ((), (), s32[]{:S(2)}) async-start(), calls=%async_computation.3 | async-start | bytes 835584 | tf_op jit(solution)/shard_map/reduce_scatter | solution.py:38
  86.6 4.2 copy-start
  92.5 1.2 copy-start.2
  93.7 538.1 %reduce-scatter.5.cloned.1.call-start = ((), (), s32[]{:S(2)}) async-start(), calls=%async_computation.2 | async-start | bytes 9584640 | tf_op jit(solution)/shard_map/reduce_scatter | solution.py:49
  166.6 213.7 %copy-start.1 = (bf16[128,192]{0,1:T(8,128)(2,1)S(1)}, bf16[128,192]{0,1:T(8,128)(2,1)}, u32[]{:S(2)}) copy-start(bf16[128,192]{0,1:T(8,128)(2,1)} %param.7) | copy-start | bytes 147460
Sparse Core Ops, SparseCore 0:
  93.8 238.9 reduce-scatter.6
  336.8 294.9 reduce-scatter.4
where the time goes:
time: 639 us
  waiting for transfers between devices  416 us (65%)
  blocking collectives  192 us (30%)
  between operations  14.1 us (2%)
  matrix products  10.9 us (2%)
    reduce_scatter x1, waiting for transfers between devices, per_device(): lax.psum_scatter(lax.dot_general(normed, grad_pre, (((0,), (0,)), ((), ()...  250 us
    reduce_scatter x1, waiting for transfers between devices, per_device(): lax.psum_scatter(rounded.astype(jnp.float32).astype(jnp.bfloat16), 'mp',...  166 us
    all_gather x1, blocking collectives, per_device(): lax.all_gather(cotangent, 'mp', axis=1, tiled=True)  79.4 us
    all_gather x1, blocking collectives, per_device(): whole = lax.all_gather(patches, 'mp', axis=1, tiled=True)  67 us
    psum x1, blocking collectives, per_device(): lax.psum((jnp.sum(grad_norm, axis=1), jnp.sum(grad_norm * unit_local, axi...  45.8 us
  transfers between devices with their start and end apart: 2, of which 2 were waited for; matrix products, arithmetic and copies ran while one was open for 1% of the time, Pallas kernels for 0%

commit v1 on v0

v1 whole, which is shorter than its diff:
```python
import math

import jax
import jax.numpy as jnp
from jax import lax
from jax.experimental import pallas as pl
from jax.experimental.pallas import tpu as pltpu
from jax.sharding import PartitionSpec as P

MESH = pl.DeviceIdType.MESH
F32 = jnp.float32
BF16 = jnp.bfloat16

NX, NY, NZ = 8, 8, 4


def gelu_slope(value):
    cdf_part = 0.5 * (1.0 + lax.erf(value * (1.0 / math.sqrt(2.0))))
    density = jnp.exp(-0.5 * value * value) * (1.0 / math.sqrt(2.0 * math.pi))
    return cdf_part + value * density


def add_bf16(a, b):
    return (a.astype(F32) + b.astype(F32)).astype(BF16)


class Counter:
    def __init__(self):
        self.n = 0

    def take(self):
        self.n += 1
        return self.n - 1


N_SEMS = 144


def kernel(
    patches, pre_act, cot, wu_hbm, wd_hbm, out_p, out_u,
    wu, wd, cbuf, nbuf, nts, slope, acc, gp, unit, q, qr, qz,
    x1, xr, zr1, z1, zr2, xr2, st1, st1r, st2, st2r,
    ssem, rsem, wsem,
):
    tok, fb = patches.shape
    d_all = fb * 2 * NY
    rb = fb // 4
    hid = pre_act.shape[1]
    cb = hid // 3
    scale = 1.0 / math.sqrt(tok * NX * NZ * 2)
    n_mp = 2 * NY
    ry, rx = NY // 2, NX // 2

    dp, mp = lax.axis_index("dp"), lax.axis_index("mp")
    c = lax.rem(dp, 2)
    x = lax.rem(dp // 2, NX)
    z = dp // (2 * NX)
    y, zh = mp // 2, lax.rem(mp, 2)

    def at_mp(off):
        return {"mp": lax.rem(mp + off, n_mp)}

    def at_y(off):
        return {"mp": lax.rem(y + off + NY, NY) * 2 + zh}

    def at_x(off):
        return {"dp": (z * NX + lax.rem(x + off + NX, NX)) * 2 + c}

    def at_z(off):
        return {"dp": (lax.rem(z + off, NZ) * NX + x) * 2 + c}

    partner = {"mp": y * 2 + 1 - zh}
    sibling = {"dp": dp + 1 - 2 * c}

    barrier = pltpu.get_barrier_semaphore()
    greeted = (
        [at_mp(k) for k in range(1, n_mp)]
        + [at_x(k) for k in range(1, NX)]
        + [at_z(k) for k in range(1, NZ)]
        + [sibling]
    )
    for peer in greeted:
        pl.semaphore_signal(barrier, inc=1, device_id=peer, device_id_type=MESH)

    load_wd = pltpu.make_async_copy(wd_hbm, wd, wsem.at[0])
    load_wu = pltpu.make_async_copy(wu_hbm, wu, wsem.at[1])
    load_wd.start()
    load_wu.start()

    counter = Counter()
    started = []

    def send(src, dst, peer):
        i = counter.take()
        copy = pltpu.make_async_remote_copy(
            src_ref=src, dst_ref=dst, send_sem=ssem.at[i], recv_sem=rsem.at[i],
            device_id=peer, device_id_type=MESH,
        )
        copy.start()
        started.append(copy)
        return copy

    cot_t = jnp.transpose(cot[...].astype(F32))
    cbuf[y, zh] = cot_t.astype(BF16).reshape(2, fb // 2, tok)
    pat_t = jnp.transpose(patches[...].astype(F32))
    total = jnp.sum(pat_t, axis=0, keepdims=True)
    off_centre = pat_t - total * (1.0 / fb)
    st1[...] = jnp.zeros_like(st1)
    st1[0:1, :] = total
    st1[1:2, :] = jnp.sum(off_centre * off_centre, axis=0, keepdims=True)
    unit[...] = pat_t
    acc[...] = jnp.zeros_like(acc)
    step = 128
    for i in range(hid // step):
        part = jnp.transpose(pre_act[:, i * step:(i + 1) * step].astype(F32))
        slope[i * step:(i + 1) * step, :] = gelu_slope(part)

    pl.semaphore_wait(barrier, len(greeted))

    def ag_start(buf, h, t):
        up, down = lax.rem(y - t + NY, NY), lax.rem(y + t, NY)
        if t < ry - 1:
            a, b = buf.at[up, h], buf.at[down, h]
        else:
            a, b = buf.at[up, h, 0], buf.at[down, h, 1]
        return send(a, a, at_y(1)), send(b, b, at_y(-1))

    stats = [send(st1, st1r.at[k - 1], at_mp(k)) for k in range(1, n_mp)]
    cot_swap = send(cbuf.at[y, zh], cbuf.at[y, zh], partner)
    cot_a = ag_start(cbuf, zh, 0)

    for copy in stats:
        copy.wait_recv()
    whole = st1[0:1, :]
    for k in range(n_mp - 1):
        whole = whole + st1r[k, 0:1, :]
    centre = whole * (1.0 / d_all)

    def block_square(sums, squares):
        shift = sums * (1.0 / fb) - centre
        return squares + fb * (shift * shift)

    square = block_square(st1[0:1, :], st1[1:2, :])
    for k in range(n_mp - 1):
        square = square + block_square(st1r[k, 0:1, :], st1r[k, 1:2, :])
    inv_std = lax.rsqrt(square * (1.0 / d_all) + 1e-06)
    unit[...] = (unit[...] - centre) * inv_std
    for par in range(2):
        for blk in range(2):
            lo = (2 * blk + par) * rb
            nts[par, blk * rb:(blk + 1) * rb, :] = unit[lo:lo + rb, :].astype(BF16)
    nbuf[y, zh, c] = nts[c]
    core_swap = send(nts.at[1 - c], nbuf.at[y, zh, c], sibling)

    cot_swap.wait_recv()
    cot_b = ag_start(cbuf, 1 - zh, 0)
    core_swap.wait_recv()
    n_swap = send(nbuf.at[y, zh], nbuf.at[y, zh], partner)
    n_a = ag_start(nbuf, zh, 0)
    load_wd.wait()

    def act_part(yp):
        lanes = pl.ds(pl.multiple_of(yp * (2 * fb), 128), 2 * fb)
        acc[...] += jnp.dot(
            wd[:, lanes], cbuf[yp].reshape(2 * fb, tok), preferred_element_type=F32
        )

    act_part(y)
    n_b = None
    for t in range(ry):
        last = t == ry - 1
        nxt = []
        for h, pair in ((zh, cot_a), (1 - zh, cot_b)):
            for copy in pair:
                copy.wait_recv()
            nxt.append(None if last else ag_start(cbuf, h, t + 1))
        cot_a, cot_b = nxt
        if not last:
            act_part(lax.rem(y - 1 - t + NY, NY))
            act_part(lax.rem(y + 1 + t, NY))
        else:
            act_part(lax.rem(y + ry, NY))
            own = (acc[...] * slope[...]).astype(BF16)
            gp[c] = own
            gp_swap = send(gp.at[c], gp.at[c], sibling)
        if t == 0:
            n_swap.wait_recv()
            n_b = ag_start(nbuf, 1 - zh, 0)
        nxt = []
        for h, pair in ((zh, n_a), (1 - zh, n_b)):
            for copy in pair:
                copy.wait_recv()
            nxt.append(None if last else ag_start(nbuf, h, t + 1))
        n_a, n_b = nxt

    load_wu.wait()
    for yp in range(NY):
        part = jnp.dot(
            wu[yp * 2 * fb:(yp + 1) * 2 * fb, :], own, preferred_element_type=F32
        )
        q[yp] = part.astype(BF16).reshape(2, fb, tok)
    far = lax.rem(y + ry, NY)
    y_up = send(q.at[far, 0], qr.at[0, 0, 0], at_y(1))
    y_down = send(q.at[far, 1], qr.at[1, 0, 1], at_y(-1))

    gp_swap.wait_recv()
    pair = jnp.concatenate([gp[0], gp[1]], axis=1)
    for yp in range(NY):
        rows = jnp.concatenate(
            [nbuf[yp, :, 0].reshape(fb, tok), nbuf[yp, :, 1].reshape(fb, tok)], axis=1
        )
        part = lax.dot_general(
            rows, pair, (((1,), (1,)), ((), ())), preferred_element_type=F32
        ).astype(BF16)
        for m in range(4):
            zp, xp = divmod(4 * yp + m, NX)
            block = part[m * rb:(m + 1) * rb, :]
            x1[0, xp, zp] = block[:, 0:cb]
            x1[1, xp, zp] = block[:, cb:2 * cb]
            z1[zp, xp] = block[:, 2 * cb:3 * cb]

    nh = NZ // 2
    xfar = lax.rem(x + rx, NX)
    x_up, x_down = [None] * 2, [None] * 2
    z_sends = []
    for s in range(2):
        x_up[s] = send(x1.at[s, xfar, pl.ds(0, nh)], xr.at[s, 0, 0, pl.ds(0, nh)], at_x(1))
        x_down[s] = send(x1.at[s, xfar, pl.ds(nh, nh)], xr.at[s, 1, 0, pl.ds(nh, nh)], at_x(-1))
    for k in range(1, NZ):
        z_sends.append(send(z1.at[lax.rem(z + k, NZ)], zr2.at[k - 1], at_z(k)))

    def y_round(t):
        up, down = lax.rem(y + ry - t, NY), lax.rem(y - ry + t + NY, NY)
        y_up.wait_recv()
        if t == 1:
            q[up, 0] = add_bf16(q[up, 0], qr[0, 0, 0])
        else:
            q[up] = add_bf16(q[up], qr[0, t - 1])
        a = send(q.at[up], qr.at[0, t], at_y(1))
        y_down.wait_recv()
        if t == 1:
            q[down, 1] = add_bf16(q[down, 1], qr[1, 0, 1])
        else:
            q[down] = add_bf16(q[down], qr[1, t - 1])
        return a, send(q.at[down], qr.at[1, t], at_y(-1))

    def x_round(s, t):
        up, down = lax.rem(x + rx - t, NX), lax.rem(x - rx + t + NX, NX)
        x_up[s].wait_recv()
        n = nh if t == 1 else NZ
        x1[s, up, 0:n] = add_bf16(x1[s, up, 0:n], xr[s, 0, t - 1, 0:n])
        x_up[s] = send(x1.at[s, up], xr.at[s, 0, t], at_x(1))
        x_down[s].wait_recv()
        n = nh if t == 1 else 0
        x1[s, down, n:NZ] = add_bf16(x1[s, down, n:NZ], xr[s, 1, t - 1, n:NZ])
        x_down[s] = send(x1.at[s, down], xr.at[s, 1, t], at_x(-1))

    for t in range(1, max(rx, ry)):
        if t < ry:
            y_up, y_down = y_round(t)
        if t < rx:
            for s in range(2):
                x_round(s, t)

    y_up.wait_recv()
    y_down.wait_recv()
    if ry == 1:
        q[y, 0] = add_bf16(q[y, 0], qr[0, 0, 0])
        q[y, 1] = add_bf16(q[y, 1], qr[1, 0, 1])
    else:
        q[y] = (
            q[y].astype(F32) + qr[0, ry - 1].astype(F32) + qr[1, ry - 1].astype(F32)
        ).astype(BF16)
    q_swap = send(q.at[y, 1 - zh], qz, partner)

    out1 = []
    for s in range(2):
        x_up[s].wait_recv()
        x_down[s].wait_recv()
        x1[s, x] = (
            x1[s, x].astype(F32) + xr[s, 0, rx - 1].astype(F32) + xr[s, 1, rx - 1].astype(F32)
        ).astype(BF16)
        out1.append(
            [send(x1.at[s, x, lax.rem(z + k, NZ)], zr1.at[s, k - 1], at_z(k)) for k in range(1, NZ)]
        )

    q_swap.wait_recv()
    grad_norm = q[y, zh].astype(F32) + qz[...].astype(F32)
    st2[...] = jnp.zeros_like(st2)
    st2[0:1, :] = jnp.sum(grad_norm, axis=0, keepdims=True)
    st2[1:2, :] = jnp.sum(grad_norm * unit[...], axis=0, keepdims=True)
    stats = [send(st2, st2r.at[k - 1], at_mp(k)) for k in range(1, n_mp)]

    for copy in z_sends:
        copy.wait_recv()
    z_sum = z1[z].astype(F32)
    for k in range(NZ - 1):
        z_sum = z_sum + zr2[k].astype(F32)
    z1[z] = z_sum.astype(BF16)
    out2 = [send(z1.at[z, lax.rem(x + k, NX)], xr2.at[k - 1], at_x(k)) for k in range(1, NX)]

    for copy in stats:
        copy.wait_recv()
    both = st2[...]
    for k in range(n_mp - 1):
        both = both + st2r[k]
    first, second = both[0:1, :] * (1.0 / d_all), both[1:2, :] * (1.0 / d_all)
    result = cbuf[y, zh].reshape(fb, tok).astype(F32) + inv_std * (
        grad_norm - first - unit[...] * second
    )
    out_p[...] = jnp.transpose(result).astype(BF16)

    for s in range(2):
        block = x1[s, x, z].astype(F32)
        for k, copy in enumerate(out1[s]):
            copy.wait_recv()
            block = block + zr1[s, k].astype(F32)
        out_u[:, s * cb:(s + 1) * cb] = block * scale
    block = z1[z, x].astype(F32)
    for k, copy in enumerate(out2):
        copy.wait_recv()
        block = block + xr2[k].astype(F32)
    out_u[:, 2 * cb:3 * cb] = block * scale

    for copy in started:
        copy.wait_send()


def per_device(patches, pre_act, cotangent, w_up, w_down):
    tok, fb = patches.shape
    hid = pre_act.shape[1]
    d_all = w_up.shape[0]
    rb, cb = fb // 4, hid // 3
    ry, rx = NY // 2, NX // 2
    vmem = pl.BlockSpec(memory_space=pltpu.VMEM)
    anywhere = pl.BlockSpec(memory_space=pl.ANY)
    return pl.pallas_call(
        kernel,
        out_shape=(
            jax.ShapeDtypeStruct((tok, fb), BF16),
            jax.ShapeDtypeStruct((rb, hid), F32),
        ),
        in_specs=[vmem, vmem, vmem, anywhere, anywhere],
        out_specs=(vmem, vmem),
        scratch_shapes=[
            pltpu.VMEM((d_all, hid), BF16),
            pltpu.VMEM((hid, d_all), BF16),
            pltpu.VMEM((NY, 2, 2, fb // 2, tok), BF16),
            pltpu.VMEM((NY, 2, 2, fb // 2, tok), BF16),
            pltpu.VMEM((2, fb // 2, tok), BF16),
            pltpu.VMEM((hid, tok), F32),
            pltpu.VMEM((hid, tok), F32),
            pltpu.VMEM((2, hid, tok), BF16),
            pltpu.VMEM((fb, tok), F32),
            pltpu.VMEM((NY, 2, fb, tok), BF16),
            pltpu.VMEM((2, ry, 2, fb, tok), BF16),
            pltpu.VMEM((fb, tok), BF16),
            pltpu.VMEM((2, NX, NZ, rb, cb), BF16),
            pltpu.VMEM((2, 2, rx, NZ, rb, cb), BF16),
            pltpu.VMEM((2, NZ - 1, rb, cb), BF16),
            pltpu.VMEM((NZ, NX, rb, cb), BF16),
            pltpu.VMEM((NZ - 1, NX, rb, cb), BF16),
            pltpu.VMEM((NX - 1, rb, cb), BF16),
            pltpu.VMEM((8, tok), F32),
            pltpu.VMEM((2 * NY - 1, 8, tok), F32),
            pltpu.VMEM((8, tok), F32),
            pltpu.VMEM((2 * NY - 1, 8, tok), F32),
            pltpu.SemaphoreType.DMA((N_SEMS,)),
            pltpu.SemaphoreType.DMA((N_SEMS,)),
            pltpu.SemaphoreType.DMA((2,)),
        ],
        compiler_params=pltpu.CompilerParams(
            collective_id=0, has_side_effects=True, vmem_limit_bytes=48 * 1024 * 1024
        ),
        cost_estimate=pl.CostEstimate(
            flops=6 * tok * d_all * hid, bytes_accessed=4 * d_all * hid, transcendentals=2 * tok * hid
        ),
    )(patches, pre_act, cotangent, w_up, w_down)


def solution(mesh):
    return jax.shard_map(
        per_device,
        mesh=mesh,
        in_specs=(P("dp", "mp"), P("dp", "mp"), P("dp", "mp"), P(None, "mp"), P("mp", None)),
        out_specs=(P("dp", "mp"), P("dp", "mp")),
        check_vma=False,
    )
```

time: 639 us -> 92.4 us (0.14)
  the two profiles are of different devices: /device:TPU:32 before, /device:TPU:128 now
where the time goes in v1:
time: 92.4 us; the launch traced here: 92.1 us
  Pallas kernels  85 us (92%)
  local copies, waits for them, and re-layouts  6.44 us (7%)
    pallas_call x1, Pallas kernels, per_device(): pl.pallas_call(kernel, out_shape=(jax.ShapeDtypeStruct((tok, fb), BF16),...  85 us
    unnamed x7, local copies, waits for them, and re-layouts  5.71 us

profile of v1, /device:TPU:128, one launch (start us, length us, event | category | flops | bytes accessed | tf_op | source)
XLA Modules:
  0.0 92.1 jit_solution(15894204046583326072)
XLA Ops:
  0.6 0.9 copy.7.patches
  1.5 0.9 copy.8.cot
  2.4 0.0 copy-start
  2.4 2.3 %copy-done = bf16[3072,768]{1,0:T(8,128)(2,1)S(1)} copy-done((bf16[3072,768]{1,0:T(8,128)(2,1)S(1)}, bf16[3072,768]{1,0:T(8,128)(2,1)}, u32[]{:S(2)}) %copy-start) | copy-done | bytes 4718616
  4.8 0.0 copy-start.1
  4.8 0.9 %copy-done.1 = bf16[128,768]{1,0:T(8,128)(2,1)S(1)} copy-done((bf16[128,768]{1,0:T(8,128)(2,1)S(1)}, bf16[128,768]{1,0:T(8,128)(2,1)}, u32[]{:S(2)}) %copy-start.1) | copy-done | bytes 196632
  5.7 85.0 %shard_map.68 = (bf16[128,192]{1,0:T(8,128)(2,1)S(1)}, f32[48,768]{1,0:T(8,128)S(1)}) custom-call(bf16[128,192]{1,0:T(8,128)(2,1)S(1)} %copy.7.patches, bf16[128,768]{1,0:T(8,128)(2,1)S(1)} %copy-done.1, bf16[128,192]{1,0:T(8,128)(2,1)S(1)} %copy.8.cot, bf16[3072,768]{1,0:T(8,128)(2,1)S(1)} %copy-done, bf16[768,3072]{1,0:T(8,128)(2,1)} %wd_hbm.1), custom_call_target="tpu_custom_call" | custom-call | flops 1811939328 | bytes 9437184 | tf_op jit(solution)/shard_map/pallas_call | solution.py:337
  90.7 0.7 copy.9
  91.4 0.7 copy.11
Async XLA Ops:
  2.4 2.3 %copy-start = (bf16[3072,768]{1,0:T(8,128)(2,1)S(1)}, bf16[3072,768]{1,0:T(8,128)(2,1)}, u32[]{:S(2)}) copy-start(bf16[3072,768]{1,0:T(8,128)(2,1)} %wu_hbm.1) | copy-start | bytes 14155780
  4.8 0.9 %copy-start.1 = (bf16[128,768]{1,0:T(8,128)(2,1)S(1)}, bf16[128,768]{1,0:T(8,128)(2,1)}, u32[]{:S(2)}) copy-start(bf16[128,768]{1,0:T(8,128)(2,1)} %pre_act.1) | copy-start | bytes 589828

commit v2 on v1

v2 whole, which is shorter than its diff:
```python
import math

import jax
import jax.numpy as jnp
from jax import lax
from jax.experimental import pallas as pl
from jax.experimental.pallas import tpu as pltpu
from jax.sharding import PartitionSpec as P

MESH = pl.DeviceIdType.MESH
F32 = jnp.float32
BF16 = jnp.bfloat16

NX, NY, NZ = 8, 8, 4


def gelu_slope(value):
    cdf_part = 0.5 * (1.0 + lax.erf(value * (1.0 / math.sqrt(2.0))))
    density = jnp.exp(-0.5 * value * value) * (1.0 / math.sqrt(2.0 * math.pi))
    return cdf_part + value * density


def add_bf16(a, b):
    return (a.astype(F32) + b.astype(F32)).astype(BF16)


class Counter:
    def __init__(self):
        self.n = 0

    def take(self):
        self.n += 1
        return self.n - 1


N_SEMS = 144


def kernel(
    patches, pre_hbm, cot, wu_hbm, wd_hbm, out_p, out_u,
    wu, wd, pre_act, cbuf, nbuf, nts, slope, acc, gp, unit, q, qr, qz,
    x1, xr, zr1, z1, zr2, xr2, st1, st1r, st2, st2r,
    ssem, rsem, wsem,
):
    fb, tok = patches.shape
    d_all = fb * 2 * NY
    rb = fb // 4
    hid = pre_act.shape[1]
    cb = hid // 3
    scale = 1.0 / math.sqrt(tok * NX * NZ * 2)
    n_mp = 2 * NY
    ry, rx = NY // 2, NX // 2

    dp, mp = lax.axis_index("dp"), lax.axis_index("mp")
    c = lax.rem(dp, 2)
    x = lax.rem(dp // 2, NX)
    z = dp // (2 * NX)
    y, zh = mp // 2, lax.rem(mp, 2)

    def at_mp(off):
        return {"mp": lax.rem(mp + off, n_mp)}

    def at_y(off):
        return {"mp": lax.rem(y + off + NY, NY) * 2 + zh}

    def at_x(off):
        return {"dp": (z * NX + lax.rem(x + off + NX, NX)) * 2 + c}

    def at_z(off):
        return {"dp": (lax.rem(z + off, NZ) * NX + x) * 2 + c}

    partner = {"mp": y * 2 + 1 - zh}
    sibling = {"dp": dp + 1 - 2 * c}

    barrier = pltpu.get_barrier_semaphore()
    greeted = (
        [at_mp(k) for k in range(1, n_mp)]
        + [at_x(k) for k in range(1, NX)]
        + [at_z(k) for k in range(1, NZ)]
        + [sibling]
    )
    for peer in greeted:
        pl.semaphore_signal(barrier, inc=1, device_id=peer, device_id_type=MESH)

    load_wd = pltpu.make_async_copy(wd_hbm, wd, wsem.at[0])
    load_wu = pltpu.make_async_copy(wu_hbm, wu, wsem.at[1])
    load_pre = pltpu.make_async_copy(pre_hbm, pre_act, wsem.at[2])
    load_pre.start()
    load_wd.start()
    load_wu.start()

    counter = Counter()
    started = []

    def send(src, dst, peer):
        i = counter.take()
        copy = pltpu.make_async_remote_copy(
            src_ref=src, dst_ref=dst, send_sem=ssem.at[i], recv_sem=rsem.at[i],
            device_id=peer, device_id_type=MESH,
        )
        copy.start()
        started.append(copy)
        return copy

    def ag_start(buf, h, t, own=None):
        up, down = lax.rem(y - t + NY, NY), lax.rem(y + t, NY)
        if t < ry - 1:
            a, b = buf.at[up, h], buf.at[down, h]
        else:
            a, b = buf.at[up, h, 0], buf.at[down, h, 1]
        if own is None:
            return send(a, a, at_y(1)), send(b, b, at_y(-1))
        if t < ry - 1:
            return send(own, a, at_y(1)), send(own, b, at_y(-1))
        return send(own.at[0], a, at_y(1)), send(own.at[1], b, at_y(-1))

    pat = patches[...].astype(F32)
    total = jnp.sum(pat, axis=0, keepdims=True)
    off_centre = pat - total * (1.0 / fb)
    st1[...] = jnp.zeros_like(st1)
    st1[0:1, :] = total
    st1[1:2, :] = jnp.sum(off_centre * off_centre, axis=0, keepdims=True)

    pl.semaphore_wait(barrier, len(greeted))

    cot_swap = send(cot, cbuf.at[y, zh], partner)
    cot_a = ag_start(cbuf, zh, 0, cot)
    stats = [send(st1, st1r.at[k - 1], at_mp(k)) for k in range(1, n_mp)]

    cbuf[y, zh] = cot[...]
    step = 128

    def slopes(lo, hi):
        for i in range(lo, hi):
            part = jnp.transpose(pre_act[:, i * step:(i + 1) * step].astype(F32))
            slope[i * step:(i + 1) * step, :] = gelu_slope(part)

    def act_part(yp, first=False):
        lanes = pl.ds(pl.multiple_of(yp * (2 * fb), 128), 2 * fb)
        part = jnp.dot(wd[:, lanes], cbuf[yp].reshape(2 * fb, tok), preferred_element_type=F32)
        acc[...] = part if first else acc[...] + part

    def act_round(t):
        if t < ry - 1:
            act_part(lax.rem(y - 1 - t + NY, NY))
            act_part(lax.rem(y + 1 + t, NY))
        else:
            act_part(lax.rem(y + ry, NY))

    def pass_on(buf, h, copies, t):
        for copy in copies:
            copy.wait_recv()
        return None if t == ry - 1 else ag_start(buf, h, t + 1)

    load_pre.wait()
    slopes(0, hid // step // 2)
    cot_a = pass_on(cbuf, zh, cot_a, 0)
    cot_swap.wait_recv()
    cot_b = ag_start(cbuf, 1 - zh, 0)
    load_wd.wait()
    act_part(y, True)
    slopes(hid // step // 2, hid // step)

    for copy in stats:
        copy.wait_recv()
    whole = st1[0:1, :]
    for k in range(n_mp - 1):
        whole = whole + st1r[k, 0:1, :]
    centre = whole * (1.0 / d_all)

    def block_square(sums, squares):
        shift = sums * (1.0 / fb) - centre
        return squares + fb * (shift * shift)

    square = block_square(st1[0:1, :], st1[1:2, :])
    for k in range(n_mp - 1):
        square = square + block_square(st1r[k, 0:1, :], st1r[k, 1:2, :])
    inv_std = lax.rsqrt(square * (1.0 / d_all) + 1e-06)
    unit[...] = (patches[...].astype(F32) - centre) * inv_std
    for par in range(2):
        for blk in range(2):
            lo = (2 * blk + par) * rb
            nts[par, blk * rb:(blk + 1) * rb, :] = unit[lo:lo + rb, :].astype(BF16)
    core_swap = send(nts.at[1 - c], nbuf.at[y, zh, c], sibling)
    nbuf[y, zh, c] = nts[c]

    n_a = n_b = n_swap = None
    n_step = 0
    for t in range(ry):
        if t > 0:
            cot_a = pass_on(cbuf, zh, cot_a, t)
        cot_b = pass_on(cbuf, 1 - zh, cot_b, t)
        if t == min(1, ry - 1):
            core_swap.wait_recv()
            n_swap = send(nbuf.at[y, zh], nbuf.at[y, zh], partner)
            n_a = ag_start(nbuf, zh, 0)
        if t == 2:
            n_a = pass_on(nbuf, zh, n_a, 0)
            n_swap.wait_recv()
            n_b = ag_start(nbuf, 1 - zh, 0)
            n_step = 1
        act_round(t)
    own = acc[...] * slope[...]
    gp[c] = jnp.transpose(own).astype(BF16)
    gp_swap = send(gp.at[c], gp.at[c], sibling)
    own = own.astype(BF16)
    if n_b is None:
        n_swap.wait_recv()
        n_b = ag_start(nbuf, 1 - zh, 0)

    def up_part(yp):
        rows = jnp.concatenate(
            [nbuf[yp, :, 0].reshape(fb, tok), nbuf[yp, :, 1].reshape(fb, tok)], axis=1
        )
        part = jnp.dot(
            rows, gp[...].reshape(2 * tok, hid), preferred_element_type=F32
        ).astype(BF16)
        for m in range(4):
            zp, xp = (4 * yp + m) // NX, lax.rem(4 * yp + m, NX)
            block = part[m * rb:(m + 1) * rb, :]
            x1[0, xp, zp] = block[:, 0:cb]
            x1[1, xp, zp] = block[:, cb:2 * cb]
            z1[zp, xp] = block[:, 2 * cb:3 * cb]

    for t in range(ry):
        if t >= n_step:
            n_a = pass_on(nbuf, zh, n_a, t)
        n_b = pass_on(nbuf, 1 - zh, n_b, t)
        if t == 0:
            gp_swap.wait_recv()
            up_part(y)
        if t < ry - 1:
            up_part(lax.rem(y - 1 - t + NY, NY))
            up_part(lax.rem(y + 1 + t, NY))
        else:
            up_part(lax.rem(y + ry, NY))

    nh = NZ // 2
    xfar = lax.rem(x + rx, NX)
    x_up, x_down = [None] * 2, [None] * 2
    z_sends = []
    for s in range(2):
        x_up[s] = send(x1.at[s, xfar, pl.ds(0, nh)], xr.at[s, 0, 0, pl.ds(0, nh)], at_x(1))
        x_down[s] = send(x1.at[s, xfar, pl.ds(nh, nh)], xr.at[s, 1, 0, pl.ds(nh, nh)], at_x(-1))
        if s == 0:
            for k in range(1, NZ):
                z_sends.append(send(z1.at[lax.rem(z + k, NZ)], zr2.at[k - 1], at_z(k)))

    load_wu.wait()
    for yp in range(NY):
        part = jnp.dot(
            wu[yp * 2 * fb:(yp + 1) * 2 * fb, :], own, preferred_element_type=F32
        )
        q[yp] = part.astype(BF16).reshape(2, fb, tok)
    far = lax.rem(y + ry, NY)
    y_up = send(q.at[far, 0], qr.at[0, 0, 0], at_y(1))
    y_down = send(q.at[far, 1], qr.at[1, 0, 1], at_y(-1))

    def y_round(t):
        up, down = lax.rem(y + ry - t, NY), lax.rem(y - ry + t + NY, NY)
        y_up.wait_recv()
        if t == 1:
            q[up, 0] = add_bf16(q[up, 0], qr[0, 0, 0])
        else:
            q[up] = add_bf16(q[up], qr[0, t - 1])
        a = send(q.at[up], qr.at[0, t], at_y(1))
        y_down.wait_recv()
        if t == 1:
            q[down, 1] = add_bf16(q[down, 1], qr[1, 0, 1])
        else:
            q[down] = add_bf16(q[down], qr[1, t - 1])
        return a, send(q.at[down], qr.at[1, t], at_y(-1))

    def x_round(s, t):
        up, down = lax.rem(x + rx - t, NX), lax.rem(x - rx + t + NX, NX)
        x_up[s].wait_recv()
        n = nh if t == 1 else NZ
        x1[s, up, 0:n] = add_bf16(x1[s, up, 0:n], xr[s, 0, t - 1, 0:n])
        x_up[s] = send(x1.at[s, up], xr.at[s, 0, t], at_x(1))
        x_down[s].wait_recv()
        n = nh if t == 1 else 0
        x1[s, down, n:NZ] = add_bf16(x1[s, down, n:NZ], xr[s, 1, t - 1, n:NZ])
        x_down[s] = send(x1.at[s, down], xr.at[s, 1, t], at_x(-1))

    def y_last():
        y_up.wait_recv()
        y_down.wait_recv()
        if ry == 1:
            q[y, 0] = add_bf16(q[y, 0], qr[0, 0, 0])
            q[y, 1] = add_bf16(q[y, 1], qr[1, 0, 1])
        else:
            q[y] = (
                q[y].astype(F32) + qr[0, ry - 1].astype(F32) + qr[1, ry - 1].astype(F32)
            ).astype(BF16)
        return send(q.at[y, 1 - zh], qz, partner)

    x_steps = [(s, t) for t in range(1, rx) for s in range(2)]
    y_steps = list(range(1, ry)) + ["last"]
    y_after = [1, 2, 3, 4]
    done = 0
    for i, (s, t) in enumerate(x_steps):
        x_round(s, t)
        if done < len(y_steps) and i >= y_after[done]:
            if y_steps[done] == "last":
                q_swap = y_last()
            else:
                y_up, y_down = y_round(y_steps[done])
            done += 1
    for step in y_steps[done:]:
        if step == "last":
            q_swap = y_last()
        else:
            y_up, y_down = y_round(step)

    out1 = []
    for s in range(2):
        x_up[s].wait_recv()
        x_down[s].wait_recv()
        x1[s, x] = (
            x1[s, x].astype(F32) + xr[s, 0, rx - 1].astype(F32) + xr[s, 1, rx - 1].astype(F32)
        ).astype(BF16)
        out1.append(
            [send(x1.at[s, x, lax.rem(z + k, NZ)], zr1.at[s, k - 1], at_z(k)) for k in range(1, NZ)]
        )

    for copy in z_sends:
        copy.wait_recv()
    z_sum = z1[z].astype(F32)
    for k in range(NZ - 1):
        z_sum = z_sum + zr2[k].astype(F32)
    z1[z] = z_sum.astype(BF16)
    out2 = [send(z1.at[z, lax.rem(x + k, NX)], xr2.at[k - 1], at_x(k)) for k in range(1, NX)]

    q_swap.wait_recv()
    grad_norm = q[y, zh].astype(F32) + qz[...].astype(F32)
    st2[...] = jnp.zeros_like(st2)
    st2[0:1, :] = jnp.sum(grad_norm, axis=0, keepdims=True)
    st2[1:2, :] = jnp.sum(grad_norm * unit[...], axis=0, keepdims=True)
    stats = [send(st2, st2r.at[k - 1], at_mp(k)) for k in range(1, n_mp)]

    for s in range(2):
        block = x1[s, x, z].astype(F32)
        for k, copy in enumerate(out1[s]):
            copy.wait_recv()
            block = block + zr1[s, k].astype(F32)
        out_u[:, s * cb:(s + 1) * cb] = block * scale

    for copy in stats:
        copy.wait_recv()
    both = st2[...]
    for k in range(n_mp - 1):
        both = both + st2r[k]
    first, second = both[0:1, :] * (1.0 / d_all), both[1:2, :] * (1.0 / d_all)
    result = cot[...].reshape(fb, tok).astype(F32) + inv_std * (
        grad_norm - first - unit[...] * second
    )
    out_p[...] = result.astype(BF16)

    block = z1[z, x].astype(F32)
    for k, copy in enumerate(out2):
        copy.wait_recv()
        block = block + xr2[k].astype(F32)
    out_u[:, 2 * cb:3 * cb] = block * scale

    for copy in started:
        copy.wait_send()


def per_device(patches, pre_act, cotangent, w_up, w_down):
    tok, fb = patches.shape
    hid = pre_act.shape[1]
    d_all = w_up.shape[0]
    rb, cb = fb // 4, hid // 3
    rx, ry = NX // 2, NY // 2
    vmem = pl.BlockSpec(memory_space=pltpu.VMEM)
    anywhere = pl.BlockSpec(memory_space=pltpu.HBM)
    grad_t, grad_up = pl.pallas_call(
        kernel,
        out_shape=(
            jax.ShapeDtypeStruct((fb, tok), BF16),
            jax.ShapeDtypeStruct((rb, hid), F32),
        ),
        in_specs=[vmem, anywhere, vmem, anywhere, anywhere],
        out_specs=(vmem, vmem),
        scratch_shapes=[
            pltpu.VMEM((d_all, hid), BF16),
            pltpu.VMEM((hid, d_all), BF16),
            pltpu.VMEM((tok, hid), BF16),
            pltpu.VMEM((NY, 2, 2, fb // 2, tok), BF16),
            pltpu.VMEM((NY, 2, 2, fb // 2, tok), BF16),
            pltpu.VMEM((2, fb // 2, tok), BF16),
            pltpu.VMEM((hid, tok), F32),
            pltpu.VMEM((hid, tok), F32),
            pltpu.VMEM((2, tok, hid), BF16),
            pltpu.VMEM((fb, tok), F32),
            pltpu.VMEM((NY, 2, fb, tok), BF16),
            pltpu.VMEM((2, ry, 2, fb, tok), BF16),
            pltpu.VMEM((fb, tok), BF16),
            pltpu.VMEM((2, NX, NZ, rb, cb), BF16),
            pltpu.VMEM((2, 2, rx, NZ, rb, cb), BF16),
            pltpu.VMEM((2, NZ - 1, rb, cb), BF16),
            pltpu.VMEM((NZ, NX, rb, cb), BF16),
            pltpu.VMEM((NZ - 1, NX, rb, cb), BF16),
            pltpu.VMEM((NX - 1, rb, cb), BF16),
            pltpu.VMEM((8, tok), F32),
            pltpu.VMEM((2 * NY - 1, 8, tok), F32),
            pltpu.VMEM((8, tok), F32),
            pltpu.VMEM((2 * NY - 1, 8, tok), F32),
            pltpu.SemaphoreType.DMA((N_SEMS,)),
            pltpu.SemaphoreType.DMA((N_SEMS,)),
            pltpu.SemaphoreType.DMA((3,)),
        ],
        compiler_params=pltpu.CompilerParams(
            collective_id=0, has_side_effects=True, vmem_limit_bytes=62 * 1024 * 1024
        ),
        cost_estimate=pl.CostEstimate(
            flops=6 * tok * d_all * hid, bytes_accessed=4 * d_all * hid, transcendentals=2 * tok * hid
        ),
    )(patches.T, pre_act, cotangent.T.reshape(2, fb // 2, tok), w_up, w_down)
    return grad_t.T, grad_up


def solution(mesh):
    return jax.shard_map(
        per_device,
        mesh=mesh,
        in_specs=(P("dp", "mp"), P("dp", "mp"), P("dp", "mp"), P(None, "mp"), P("mp", None)),
        out_specs=(P("dp", "mp"), P("dp", "mp")),
        check_vma=False,
    )
```

time: 92.4 us -> 94 us (1.017)
  the two profiles are of different devices: /device:TPU:128 before, /device:TPU:6 now
where the time goes in v2:
time: 94 us; the launch traced here: 93.7 us
  Pallas kernels  90.1 us (96%)
  local copies, waits for them, and re-layouts  3 us (3%)
    pallas_call x1, Pallas kernels, per_device(): pl.pallas_call(kernel, out_shape=(jax.ShapeDtypeStruct((fb, tok), BF16),...  90.1 us
    unnamed x2, local copies, waits for them, and re-layouts  3 us

profile of v2, /device:TPU:6, one launch (start us, length us, event | category | flops | bytes accessed | tf_op | source)
XLA Modules:
  0.0 93.7 jit_solution(12779546938421553950)
XLA Ops:
  0.6 90.1 %shard_map.68 = (bf16[192,128]{1,0:T(8,128)(2,1)}, f32[48,768]{1,0:T(8,128)}) custom-call(bf16[192,128]{1,0:T(8,128)(2,1)} %bitcast.5, bf16[128,768]{1,0:T(8,128)(2,1)} %pre_hbm.1, bf16[2,96,128]{2,1,0:T(8,128)(2,1)} %bitcast.6, bf16[3072,768]{1,0:T(8,128)(2,1)} %wu_hbm.1, bf16[768,3072]{1,0:T(8,128)(2,1)} %wd_hbm.1), custom_call_target="tpu_custom_call" | custom-call | flops 1811939328 | bytes 9437184 | tf_op jit(solution)/shard_map/pallas_call | solution.py:377
  90.7 1.4 %copy.9 = bf16[128,192]{0,1:T(8,128)(2,1)} copy(bf16[128,192]{0,1:T(8,128)(2,1)} %bitcast.7) | data formatting | bytes 98304
  92.1 1.6 %copy.10 = f32[48,768]{1,0:T(8,128)} copy(f32[48,768]{1,0:T(8,128)} %get-tuple-element.9) | data formatting | bytes 294912

commit v3 on v2

v3 whole, which is shorter than its diff:
```python
import math

import jax
import jax.numpy as jnp
from jax import lax
from jax.experimental import pallas as pl
from jax.experimental.pallas import tpu as pltpu
from jax.sharding import PartitionSpec as P

MESH = pl.DeviceIdType.MESH
F32 = jnp.float32
BF16 = jnp.bfloat16

NX, NY, NZ = 8, 8, 4


def gelu_slope(value):
    cdf_part = 0.5 * (1.0 + lax.erf(value * (1.0 / math.sqrt(2.0))))
    density = jnp.exp(-0.5 * value * value) * (1.0 / math.sqrt(2.0 * math.pi))
    return cdf_part + value * density


def add_bf16(a, b):
    return (a.astype(F32) + b.astype(F32)).astype(BF16)


class Counter:
    def __init__(self):
        self.n = 0

    def take(self):
        self.n += 1
        return self.n - 1


N_SEMS = 144


def kernel(
    patches, pre_hbm, cot, wu_hbm, wd_hbm, out_p, out_u,
    wu, wd, pre_act, cbuf, nbuf, pats, pbuf, slope, acc, gp, unit, q, qr, qz, qsum,
    x1, xr, zr1, z1, zr2, xr2, lnp, st1, st1r, st2, st2r, st3, st3r,
    ssem, rsem, wsem,
):
    fb, tok = patches.shape
    d_all = fb * 2 * NY
    rb = fb // 4
    hid = pre_act.shape[1]
    cb = hid // 3
    scale = 1.0 / math.sqrt(tok * NX * NZ * 2)
    ry, rx = NY // 2, NX // 2

    dp, mp = lax.axis_index("dp"), lax.axis_index("mp")
    c = lax.rem(dp, 2)
    x = lax.rem(dp // 2, NX)
    z = dp // (2 * NX)
    y, zh = mp // 2, lax.rem(mp, 2)

    def at_y(off):
        return {"mp": lax.rem(y + off + NY, NY) * 2 + zh}

    def at_x(off):
        return {"dp": (z * NX + lax.rem(x + off + NX, NX)) * 2 + c}

    def at_z(off):
        return {"dp": (lax.rem(z + off, NZ) * NX + x) * 2 + c}

    partner = {"mp": y * 2 + 1 - zh}
    sibling = {"dp": dp + 1 - 2 * c}

    barrier = pltpu.get_barrier_semaphore()
    greeted = (
        [at_y(k) for k in range(1, NY)]
        + [at_x(k) for k in range(1, NX)]
        + [at_z(k) for k in range(1, NZ)]
        + [sibling, partner]
    )
    for peer in greeted:
        pl.semaphore_signal(barrier, inc=1, device_id=peer, device_id_type=MESH)

    def loads(src, dst, first):
        n = src.shape[0] // 4
        return [
            pltpu.make_async_copy(
                src.at[pl.ds(i * n, n)], dst.at[pl.ds(i * n, n)], wsem.at[first + i]
            )
            for i in range(4)
        ]

    load_pre = pltpu.make_async_copy(pre_hbm, pre_act, wsem.at[8])
    load_wd, load_wu = loads(wd_hbm, wd, 0), loads(wu_hbm, wu, 4)
    for copy in [load_pre] + load_wd:
        copy.start()

    counter = Counter()
    started = []

    def send(src, dst, peer):
        i = counter.take()
        copy = pltpu.make_async_remote_copy(
            src_ref=src, dst_ref=dst, send_sem=ssem.at[i], recv_sem=rsem.at[i],
            device_id=peer, device_id_type=MESH,
        )
        copy.start()
        started.append(copy)
        return copy

    def ag_start(buf, h, t, own=None):
        up, down = lax.rem(y - t + NY, NY), lax.rem(y + t, NY)
        if t < ry - 1:
            a, b = buf.at[up, h], buf.at[down, h]
        else:
            a, b = buf.at[up, h, 0], buf.at[down, h, 1]
        if own is None:
            return send(a, a, at_y(1)), send(b, b, at_y(-1))
        if t < ry - 1:
            return send(own, a, at_y(1)), send(own, b, at_y(-1))
        return send(own.at[0], a, at_y(1)), send(own.at[1], b, at_y(-1))

    for par in range(2):
        for blk in range(2):
            lo = (2 * blk + par) * rb
            pats[par, blk * rb:(blk + 1) * rb, :] = patches[lo:lo + rb, :]

    pl.semaphore_wait(barrier, len(greeted))

    cot_swap = send(cot, cbuf.at[y, zh], partner)
    core_swap = send(pats.at[1 - c], nbuf.at[y, zh, c], sibling)
    cot_a = ag_start(cbuf, zh, 0, cot)
    pat_swap = [send(pats.at[c], nbuf.at[y, zh, c], partner)]
    nbuf[y, zh, c] = pats[c]

    cbuf[y, zh] = cot[...]
    step = 128

    def slopes(lo, hi):
        for i in range(lo, hi):
            part = jnp.transpose(pre_act[:, i * step:(i + 1) * step].astype(F32))
            slope[i * step:(i + 1) * step, :] = gelu_slope(part)

    def act_part(yp, first=False):
        lanes = pl.ds(pl.multiple_of(yp * (2 * fb), 128), 2 * fb)
        part = jnp.dot(wd[:, lanes], cbuf[yp].reshape(2 * fb, tok), preferred_element_type=F32)
        acc[...] = part if first else acc[...] + part

    def act_round(t):
        if t < ry - 1:
            act_part(lax.rem(y - 1 - t + NY, NY))
            act_part(lax.rem(y + 1 + t, NY))
        else:
            act_part(lax.rem(y + ry, NY))

    def pass_on(buf, h, copies, t):
        for copy in copies:
            copy.wait_recv()
        return None if t == ry - 1 else ag_start(buf, h, t + 1)

    def norm_part(yp):
        for k in range(2):
            block = nbuf[yp, :, k].reshape(fb, tok).astype(F32)
            total = jnp.sum(block, axis=0, keepdims=True)
            off = block - total * (1.0 / fb)
            lnp[yp, k:k + 1, :] = total
            lnp[yp, 2 + k:3 + k, :] = jnp.sum(off * off, axis=0, keepdims=True)

    def norm_round(t):
        if t < ry - 1:
            norm_part(lax.rem(y - 1 - t + NY, NY))
            norm_part(lax.rem(y + 1 + t, NY))
        else:
            norm_part(lax.rem(y + ry, NY))

    core_swap.wait_recv()
    pat_swap.append(send(nbuf.at[y, zh, 1 - c], nbuf.at[y, zh, 1 - c], partner))
    pat_a = ag_start(nbuf, zh, 0)
    load_pre.wait()
    slopes(0, hid // step)
    for t in range(ry + 1):
        if t < ry:
            cot_a = pass_on(cbuf, zh, cot_a, t)
            pat_a = pass_on(nbuf, zh, pat_a, t)
        if t == 0:
            cot_swap.wait_recv()
            cot_b = ag_start(cbuf, 1 - zh, 0)
            for copy in pat_swap:
                copy.wait_recv()
            pat_b = ag_start(nbuf, 1 - zh, 0)
            other_rows = send(nbuf.at[y, 1 - zh, 1 - c], pbuf, sibling)
            norm_part(y)
        else:
            cot_b = pass_on(cbuf, 1 - zh, cot_b, t - 1)
            if t < ry:
                pat_b = pass_on(nbuf, 1 - zh, pat_b, t - 1)
            if t == 1:
                for copy in load_wd:
                    copy.wait()
                for copy in load_wu:
                    copy.start()
                act_part(y, True)
            if t < ry:
                act_round(t - 1)
                norm_round(t - 1)
    act_round(ry - 1)
    own = acc[...] * slope[...]
    gp[c] = jnp.transpose(own).astype(BF16)
    gp_swap = send(gp.at[c], gp.at[c], sibling)
    own = own.astype(BF16)
    pass_on(nbuf, 1 - zh, pat_b, ry - 1)
    norm_round(ry - 1)

    def combine(parts, count):
        whole = parts[0][0]
        for sums, _ in parts[1:]:
            whole = whole + sums
        mean = whole * (1.0 / (count * len(parts)))
        square = None
        for sums, squares in parts:
            shift = sums * (1.0 / count) - mean
            term = squares + count * (shift * shift)
            square = term if square is None else square + term
        return whole, square

    here = combine([(lnp[yp, 0:2, :], lnp[yp, 2:4, :]) for yp in range(NY)], fb)
    st1[...] = jnp.zeros_like(st1)
    st1[0:2, :], st1[2:4, :] = here
    norm_swap = send(st1, st1r, sibling)

    for copy in load_wu:
        copy.wait()
    for yp in range(NY):
        part = jnp.dot(
            wu[yp * 2 * fb:(yp + 1) * 2 * fb, :], own, preferred_element_type=F32
        )
        q[yp] = part.astype(BF16).reshape(2, fb, tok)
    far = lax.rem(y + ry, NY)
    y_up = send(q.at[far, 0], qr.at[0, 0, 0], at_y(1))
    y_down = send(q.at[far, 1], qr.at[1, 0, 1], at_y(-1))

    norm_swap.wait_recv()
    whole, square = combine([here, (st1r[0:2, :], st1r[2:4, :])], d_all // 2)
    centres = whole * (1.0 / d_all)
    inv_stds = lax.rsqrt(square * (1.0 / d_all) + 1e-06)
    centre = jnp.where(c == 0, centres[0:1, :], centres[1:2, :])
    inv_std = jnp.where(c == 0, inv_stds[0:1, :], inv_stds[1:2, :])

    def up_part(yp):
        rows = [
            (nbuf[yp, :, k].reshape(fb, tok).astype(F32) - centres[k:k + 1, :])
            * inv_stds[k:k + 1, :]
            for k in range(2)
        ]
        part = jnp.dot(
            jnp.concatenate(rows, axis=1).astype(BF16),
            gp[...].reshape(2 * tok, hid),
            preferred_element_type=F32,
        ).astype(BF16)
        for m in range(4):
            zp, xp = divmod(4 * yp + m, NX)
            block = part[m * rb:(m + 1) * rb, :]
            x1[0, xp, zp] = block[:, 0:cb]
            x1[1, xp, zp] = block[:, cb:2 * cb]
            z1[zp, xp] = block[:, 2 * cb:3 * cb]

    gp_swap.wait_recv()
    for yp in range(NY):
        up_part(yp)

    nh = NZ // 2
    xfar = lax.rem(x + rx, NX)
    x_up, x_down = [None] * 2, [None] * 2
    z_sends = []
    for s in range(2):
        x_up[s] = send(x1.at[s, xfar, pl.ds(0, nh)], xr.at[s, 0, 0, pl.ds(0, nh)], at_x(1))
        x_down[s] = send(x1.at[s, xfar, pl.ds(nh, nh)], xr.at[s, 1, 0, pl.ds(nh, nh)], at_x(-1))
        if s == 0:
            for k in range(1, NZ):
                z_sends.append(send(z1.at[lax.rem(z + k, NZ)], zr2.at[k - 1], at_z(k)))

    def y_round(t):
        up, down = lax.rem(y + ry - t, NY), lax.rem(y - ry + t + NY, NY)
        y_up.wait_recv()
        if t == 1:
            q[up, 0] = add_bf16(q[up, 0], qr[0, 0, 0])
        else:
            q[up] = add_bf16(q[up], qr[0, t - 1])
        a = send(q.at[up], qr.at[0, t], at_y(1))
        y_down.wait_recv()
        if t == 1:
            q[down, 1] = add_bf16(q[down, 1], qr[1, 0, 1])
        else:
            q[down] = add_bf16(q[down], qr[1, t - 1])
        return a, send(q.at[down], qr.at[1, t], at_y(-1))

    def x_round(s, t):
        up, down = lax.rem(x + rx - t, NX), lax.rem(x - rx + t + NX, NX)
        x_up[s].wait_recv()
        n = nh if t == 1 else NZ
        x1[s, up, 0:n] = add_bf16(x1[s, up, 0:n], xr[s, 0, t - 1, 0:n])
        x_up[s] = send(x1.at[s, up], xr.at[s, 0, t], at_x(1))
        x_down[s].wait_recv()
        n = nh if t == 1 else 0
        x1[s, down, n:NZ] = add_bf16(x1[s, down, n:NZ], xr[s, 1, t - 1, n:NZ])
        x_down[s] = send(x1.at[s, down], xr.at[s, 1, t], at_x(-1))

    def unit_of(block):
        return (block.astype(F32) - centre) * inv_std

    def y_last():
        y_up.wait_recv()
        y_down.wait_recv()
        if ry == 1:
            qsum[0] = q[y, 0].astype(F32) + qr[0, 0, 0].astype(F32)
            qsum[1] = q[y, 1].astype(F32) + qr[1, 0, 1].astype(F32)
        else:
            qsum[...] = (
                q[y].astype(F32) + qr[0, ry - 1].astype(F32) + qr[1, ry - 1].astype(F32)
            )
        q[y, 1 - zh] = qsum[1 - zh].astype(BF16)
        swap = send(q.at[y, 1 - zh], qz, partner)
        first = jnp.sum(qsum[0] + qsum[1], axis=0, keepdims=True)
        second = jnp.sum(qsum[zh] * unit[...], axis=0, keepdims=True)
        for par, rows in ((c, nbuf[y, 1 - zh, c]), (1 - c, pbuf[...])):
            for blk in range(2):
                lo = pl.multiple_of((2 * blk + par) * rb, rb)
                second = second + jnp.sum(
                    qsum[1 - zh, pl.ds(lo, rb), :] * unit_of(rows[blk * rb:(blk + 1) * rb, :]),
                    axis=0,
                    keepdims=True,
                )
        st2[...] = jnp.zeros_like(st2)
        st2[0:1, :] = first
        st2[1:2, :] = second
        return swap, [send(st2, st2r.at[k - 1], at_y(k)) for k in range(1, NY)]

    out1 = [None] * 2

    def x_last(s):
        x_up[s].wait_recv()
        x_down[s].wait_recv()
        x1[s, x] = (
            x1[s, x].astype(F32) + xr[s, 0, rx - 1].astype(F32) + xr[s, 1, rx - 1].astype(F32)
        ).astype(BF16)
        out1[s] = [
            send(x1.at[s, x, lax.rem(z + k, NZ)], zr1.at[s, k - 1], at_z(k)) for k in range(1, NZ)
        ]

    unit[...] = unit_of(patches[...])
    other_rows.wait_recv()
    for t in range(1, max(rx, ry)):
        if t < ry:
            y_up, y_down = y_round(t)
        if t < rx:
            for s in range(2):
                x_round(s, t)
    q_swap, stats = y_last()

    x_last(0)
    for copy in z_sends:
        copy.wait_recv()
    z_sum = z1[z].astype(F32)
    for k in range(NZ - 1):
        z_sum = z_sum + zr2[k].astype(F32)
    z1[z] = z_sum.astype(BF16)
    out2 = [send(z1.at[z, lax.rem(x + k, NX)], xr2.at[k - 1], at_x(k)) for k in range(1, NX)]
    for copy in stats:
        copy.wait_recv()
    both = st2[...]
    for k in range(NY - 1):
        both = both + st2r[k]
    st3[...] = both
    stats = send(st3, st3r, partner)
    x_last(1)

    q_swap.wait_recv()
    grad_norm = qsum[zh] + qz[...].astype(F32)
    stats.wait_recv()
    both = st3[...] + st3r[...]
    first, second = both[0:1, :] * (1.0 / d_all), both[1:2, :] * (1.0 / d_all)
    result = cot[...].reshape(fb, tok).astype(F32) + inv_std * (
        grad_norm - first - unit[...] * second
    )
    out_p[...] = result.astype(BF16)

    for s in range(2):
        block = x1[s, x, z].astype(F32)
        for k, copy in enumerate(out1[s]):
            copy.wait_recv()
            block = block + zr1[s, k].astype(F32)
        out_u[:, s * cb:(s + 1) * cb] = block * scale

    block = z1[z, x].astype(F32)
    for k, copy in enumerate(out2):
        copy.wait_recv()
        block = block + xr2[k].astype(F32)
    out_u[:, 2 * cb:3 * cb] = block * scale

    for copy in started:
        copy.wait_send()


def per_device(patches, pre_act, cotangent, w_up, w_down):
    tok, fb = patches.shape
    hid = pre_act.shape[1]
    d_all = w_up.shape[0]
    rb, cb = fb // 4, hid // 3
    rx, ry = NX // 2, NY // 2
    vmem = pl.BlockSpec(memory_space=pltpu.VMEM)
    anywhere = pl.BlockSpec(memory_space=pltpu.HBM)
    grad_t, grad_up = pl.pallas_call(
        kernel,
        out_shape=(
            jax.ShapeDtypeStruct((fb, tok), BF16),
            jax.ShapeDtypeStruct((rb, hid), F32),
        ),
        in_specs=[vmem, anywhere, vmem, anywhere, anywhere],
        out_specs=(vmem, vmem),
        scratch_shapes=[
            pltpu.VMEM((d_all, hid), BF16),
            pltpu.VMEM((hid, d_all), BF16),
            pltpu.VMEM((tok, hid), BF16),
            pltpu.VMEM((NY, 2, 2, fb // 2, tok), BF16),
            pltpu.VMEM((NY, 2, 2, fb // 2, tok), BF16),
            pltpu.VMEM((2, fb // 2, tok), BF16),
            pltpu.VMEM((fb // 2, tok), BF16),
            pltpu.VMEM((hid, tok), F32),
            pltpu.VMEM((hid, tok), F32),
            pltpu.VMEM((2, tok, hid), BF16),
            pltpu.VMEM((fb, tok), F32),
            pltpu.VMEM((NY, 2, fb, tok), BF16),
            pltpu.VMEM((2, ry, 2, fb, tok), BF16),
            pltpu.VMEM((fb, tok), BF16),
            pltpu.VMEM((2, fb, tok), F32),
            pltpu.VMEM((2, NX, NZ, rb, cb), BF16),
            pltpu.VMEM((2, 2, rx, NZ, rb, cb), BF16),
            pltpu.VMEM((2, NZ - 1, rb, cb), BF16),
            pltpu.VMEM((NZ, NX, rb, cb), BF16),
            pltpu.VMEM((NZ - 1, NX, rb, cb), BF16),
            pltpu.VMEM((NX - 1, rb, cb), BF16),
            pltpu.VMEM((NY, 8, tok), F32),
            pltpu.VMEM((8, tok), F32),
            pltpu.VMEM((8, tok), F32),
            pltpu.VMEM((8, tok), F32),
            pltpu.VMEM((NY - 1, 8, tok), F32),
            pltpu.VMEM((8, tok), F32),
            pltpu.VMEM((8, tok), F32),
            pltpu.SemaphoreType.DMA((N_SEMS,)),
            pltpu.SemaphoreType.DMA((N_SEMS,)),
            pltpu.SemaphoreType.DMA((9,)),
        ],
        compiler_params=pltpu.CompilerParams(
            collective_id=0, has_side_effects=True, vmem_limit_bytes=62 * 1024 * 1024
        ),
        cost_estimate=pl.CostEstimate(
            flops=6 * tok * d_all * hid, bytes_accessed=4 * d_all * hid, transcendentals=2 * tok * hid
        ),
    )(patches.T, pre_act, cotangent.T.reshape(2, fb // 2, tok), w_up, w_down)
    return grad_t.T, grad_up


def solution(mesh):
    return jax.shard_map(
        per_device,
        mesh=mesh,
        in_specs=(P("dp", "mp"), P("dp", "mp"), P("dp", "mp"), P(None, "mp"), P("mp", None)),
        out_specs=(P("dp", "mp"), P("dp", "mp")),
        check_vma=False,
    )
```

time: 94 us -> 80.2 us (0.85)
  the two profiles are of different devices: /device:TPU:6 before, /device:TPU:160 now
where the time goes in v3:
time: 80.2 us; the launch traced here: 79.9 us
  Pallas kernels  76.3 us (95%)
  local copies, waits for them, and re-layouts  3 us (4%)
    pallas_call x1, Pallas kernels, per_device(): pl.pallas_call(kernel, out_shape=(jax.ShapeDtypeStruct((fb, tok), BF16),...  76.3 us
    unnamed x2, local copies, waits for them, and re-layouts  3 us

profile of v3, /device:TPU:160, one launch (start us, length us, event | category | flops | bytes accessed | tf_op | source)
XLA Modules:
  0.0 79.9 jit_solution(12390705859817975772)
XLA Ops:
  0.6 76.3 %shard_map.68 = (bf16[192,128]{1,0:T(8,128)(2,1)}, f32[48,768]{1,0:T(8,128)}) custom-call(bf16[192,128]{1,0:T(8,128)(2,1)} %bitcast.5, bf16[128,768]{1,0:T(8,128)(2,1)} %pre_hbm.1, bf16[2,96,128]{2,1,0:T(8,128)(2,1)} %bitcast.6, bf16[3072,768]{1,0:T(8,128)(2,1)} %wu_hbm.1, bf16[768,3072]{1,0:T(8,128)(2,1)} %wd_hbm.1), custom_call_target="tpu_custom_call" | custom-call | flops 1811939328 | bytes 9437184 | tf_op jit(solution)/shard_map/pallas_call | solution.py:409
  76.9 1.4 %copy.9 = bf16[128,192]{0,1:T(8,128)(2,1)} copy(bf16[128,192]{0,1:T(8,128)(2,1)} %bitcast.7) | data formatting | bytes 98304
  78.3 1.6 %copy.10 = f32[48,768]{1,0:T(8,128)} copy(f32[48,768]{1,0:T(8,128)} %get-tuple-element.9) | data formatting | bytes 294912

commit v4 on v3

--- a/solution.py
+++ b/solution.py
@@ -265,6 +265,7 @@
     for yp in range(NY):
         up_part(yp)
 
+    gathered = len(started)
     nh = NZ // 2
     xfar = lax.rem(x + rx, NX)
     x_up, x_down = [None] * 2, [None] * 2
@@ -352,6 +353,9 @@
         if t < rx:
             for s in range(2):
                 x_round(s, t)
+    for copy in started[:gathered]:
+        copy.wait_send()
+    reduced = len(started)
     q_swap, stats = y_last()
 
     x_last(0)
@@ -370,6 +374,8 @@
     st3[...] = both
     stats = send(st3, st3r, partner)
     x_last(1)
+    for copy in started[gathered:reduced]:
+        copy.wait_send()
 
     q_swap.wait_recv()
     grad_norm = qsum[zh] + qz[...].astype(F32)
@@ -394,7 +400,7 @@
         block = block + xr2[k].astype(F32)
     out_u[:, 2 * cb:3 * cb] = block * scale
 
-    for copy in started:
+    for copy in started[reduced:]:
         copy.wait_send()
 
 

time: 80.2 us -> 80.1 us (level)
  no operation moved by 1% of the time
where the time goes in v4:
time: 80.1 us; the launch traced here: 79.8 us
  Pallas kernels  76.2 us (95%)
  local copies, waits for them, and re-layouts  3 us (4%)
    pallas_call x1, Pallas kernels, per_device(): pl.pallas_call(kernel, out_shape=(jax.ShapeDtypeStruct((fb, tok), BF16),...  76.2 us
    unnamed x2, local copies, waits for them, and re-layouts  3 us

profile of v4, /device:TPU:160, one launch (start us, length us, event | category | flops | bytes accessed | tf_op | source)
XLA Modules:
  0.0 79.8 jit_solution(4957512548651712816)
XLA Ops:
  0.6 76.2 %shard_map.68 = (bf16[192,128]{1,0:T(8,128)(2,1)}, f32[48,768]{1,0:T(8,128)}) custom-call(bf16[192,128]{1,0:T(8,128)(2,1)} %bitcast.5, bf16[128,768]{1,0:T(8,128)(2,1)} %pre_hbm.1, bf16[2,96,128]{2,1,0:T(8,128)(2,1)} %bitcast.6, bf16[3072,768]{1,0:T(8,128)(2,1)} %wu_hbm.1, bf16[768,3072]{1,0:T(8,128)(2,1)} %wd_hbm.1), custom_call_target="tpu_custom_call" | custom-call | flops 1811939328 | bytes 9437184 | tf_op jit(solution)/shard_map/pallas_call | solution.py:415
  76.8 1.4 %copy.9 = bf16[128,192]{0,1:T(8,128)(2,1)} copy(bf16[128,192]{0,1:T(8,128)(2,1)} %bitcast.7) | data formatting | bytes 98304
  78.2 1.6 %copy.10 = f32[48,768]{1,0:T(8,128)} copy(f32[48,768]{1,0:T(8,128)} %get-tuple-element.9) | data formatting | bytes 294912
